TPU v7x, 256 devices: a whole 4x4x8 slice. The times are simulated.
256 devices in a mesh: row: 32 (over y, z_lo, core), col: 8 (over z_hi, x).
Axes of the slice: x: 4, y: 4, z: 8 (z_hi: 2, z_lo: 4; z = z_hi * 4 + z_lo), core: 2. Of those that a mesh axis runs over, the one named last changes fastest.
Arguments:
- views: bfloat16 [81, 2048, 2048], P(None, 'row', 'col'), may hold values from -6 to 6
Outputs:
- increment: float32 [2048, 2048], P('row', 'col')
- residual: float32 [2048, 2048], P('row', 'col')
All inputs are finite; a program needn't handle non-finite values.
Results may differ from a plain program's by a relative error of at most 0.0005.
Values may be sent and summed in bfloat16 or wider, within the bound.
No kernel may reach another device: no remote copies, remote signals or barrier semaphores. Data moves between devices by JAX's collectives and lax.ppermute only.
A program may use at most 64 MiB of HBM per device.

v0:
```python
import jax
import jax.numpy as jnp
from jax import lax
from jax.sharding import Mesh
from jax.sharding import PartitionSpec as P

ANG = 9
VIEWS = 81
D0 = 3
HALO = 13
ITERS = 2
ROW_COL = ("row_0", "row_1", "row_2", "col_0", "col_1")
ROW = ("row_0", "row_1", "row_2")
COL = ("col_0", "col_1")
smooth_weight = 2.0
damping = 0.1


def with_halo(array, sides, width):
    for axis, dim in sides:
        count, length = (lax.axis_size(axis), array.shape[dim])
        up = [(i, (i + 1) % count) for i in range(count - 1)]
        down = [(j, i) for i, j in up]
        last = lax.slice_in_dim(array, length - width, length, axis=dim)
        leading = lax.slice_in_dim(array, 0, width, axis=dim)
        before = lax.ppermute(last, axis, up)
        after = lax.ppermute(leading, axis, down)
        array = jnp.concatenate([before, array, after], axis=dim)
    return array


def by_axis(array, axes):
    for axis in axes:
        array = lax.psum(array, axis)
    return array


def operate(field, coeff, horiz, verti):
    padded = with_halo(field, ((ROW, 0), (COL, 1)), 1)
    edges = horiz[:, 1:] * (field - padded[1:-1, 2:]) + horiz[:, :-1] * (field - padded[1:-1, :-2])
    edges = (
        edges + verti[1:] * (field - padded[2:, 1:-1]) + verti[:-1] * (field - padded[:-2, 1:-1])
    )
    return coeff * field + smooth_weight * edges


def row_band(col_ext, srow_index, rows_dev):
    srow = srow_index - ANG // 2
    reach = D0 * abs(srow) + 1
    block = col_ext[srow_index * ANG : (srow_index + 1) * ANG]
    grown = with_halo(block, ((ROW, 1),), reach)
    start = reach + D0 * srow - 1
    return grown[:, start : start + rows_dev + 2, :]


def shards(views):
    rows_dev = views.shape[1]
    cols_dev = views.shape[2]
    total_rows = rows_dev * lax.axis_size(ROW)
    total_cols = cols_dev * lax.axis_size(COL)
    bands = []
    col_ext = with_halo(views, ((COL, 2),), HALO)
    for srow_index in range(ANG):
        bands.append(row_band(col_ext, srow_index, rows_dev))
    center_ext = bands[ANG // 2][ANG // 2, :, HALO - 1 : HALO + cols_dev + 1].astype(jnp.float32)
    center = center_ext[1:-1, 1:-1]
    data_sum = jnp.zeros((rows_dev, cols_dev), jnp.float32)
    source_sum = jnp.zeros((rows_dev, cols_dev), jnp.float32)
    for srow_index in range(ANG):
        srow = float(srow_index - ANG // 2)
        band = bands[srow_index]
        for tindex in range(ANG):
            tcol = tindex - ANG // 2
            left = HALO + D0 * tcol
            image = band[tindex].astype(jnp.float32)
            warped = image[1:-1, left : left + cols_dev]
            down_diff = 0.5 * (
                image[2:, left : left + cols_dev] - image[:-2, left : left + cols_dev]
            )
            side_diff = 0.5 * (
                image[1:-1, left + 1 : left + 1 + cols_dev]
                - image[1:-1, left - 1 : left - 1 + cols_dev]
            )
            slope = srow * down_diff + tcol * side_diff
            error = warped - center
            robust = 1.0 / jnp.sqrt(1.0 + error * error)
            data_sum = data_sum + robust * slope * slope
            source_sum = source_sum - robust * slope * error
    coeff = damping + data_sum / VIEWS
    source = source_sum / VIEWS
    across = center_ext[1:-1, 1:] - center_ext[1:-1, :-1]
    vertical = center_ext[1:, 1:-1] - center_ext[:-1, 1:-1]
    columns = lax.axis_index(COL) * cols_dev + jnp.arange(cols_dev + 1)
    row_index = lax.axis_index(ROW) * rows_dev + jnp.arange(rows_dev + 1)
    horiz = jnp.where(
        ((columns >= 1) & (columns <= total_cols - 1))[None, :], jnp.exp(-across * across), 0.0
    )
    verti = jnp.where(
        ((row_index >= 1) & (row_index <= total_rows - 1))[:, None],
        jnp.exp(-vertical * vertical),
        0.0,
    )
    precond = coeff + smooth_weight * (horiz[:, 1:] + horiz[:, :-1] + verti[1:] + verti[:-1])
    solution = jnp.zeros_like(source)
    residual = source
    scaled_res = residual / precond
    image_res = operate(scaled_res, coeff, horiz, verti)
    inner_old = None
    step_old = None
    for step in range(ITERS):
        inner_rz, inner_wu = (
            by_axis(jnp.sum(residual * scaled_res), ROW_COL),
            by_axis(jnp.sum(image_res * scaled_res), ROW_COL),
        )
        scaled_img = image_res / precond
        last_step = step + 1 == ITERS
        if not last_step:
            next_image = operate(scaled_img, coeff, horiz, verti)
        if step == 0:
            step_size = inner_rz / inner_wu
            direction = scaled_res
            dir_image = image_res
            dir_scaled = scaled_img
            dir_second = next_image
        else:
            momentum = inner_rz / inner_old
            step_size = inner_rz / (inner_wu - momentum * inner_rz / step_old)
            direction = scaled_res + momentum * direction
            dir_image = image_res + momentum * dir_image
        solution = solution + step_size * direction
        residual = residual - step_size * dir_image
        if not last_step:
            scaled_res = scaled_res - step_size * dir_scaled
            image_res = image_res - step_size * dir_second
        inner_old = inner_rz
        step_old = step_size
    return (solution, residual)


def solution(mesh):
    finer = Mesh(mesh.devices.reshape(4, 4, 2, 2, 4), ("row_0", "row_1", "row_2", "col_0", "col_1"))
    in_specs = (P(None, ROW, COL),)
    out_specs = (P(ROW, COL), P(ROW, COL))
    return jax.shard_map(
        shards, mesh=finer, in_specs=in_specs, out_specs=out_specs, check_vma=False
    )
```

profile of v0, /device:TPU:10, one launch (start us, length us, event | category | flops | bytes accessed | tf_op | source)
XLA Modules:
  0.0 256.1 jit_solution(15290785969575630049)
XLA Ops:
  0.6 3.4 %fusion.427 = (bf16[81,64,13]{2,1,0:T(8,128)(2,1)}, bf16[81,64,13]{2,1,0:T(8,128)(2,1)S(1)}) fusion(bf16[81,64,256]{2,1,0:T(8,128)(2,1)} %param.1), kind=kLoop, calls=%fused_computation.861 | loop fusion | bytes 539136 | tf_op jit(solution)/shard_map/slice | solution.py:24
  5.8 2.7 %collective-permute-start.1 = (bf16[81,64,13]{0,1,2:T(8,128)(2,1)S(1)}, bf16[81,64,13]{0,1,2:T(8,128)(2,1)S(1)}, u32[]{:S(2)}, u32[]{:S(2)}) collective-permute-start(bf16[81,64,13]{0,1,2:T(8,128)(2,1)S(1)} %copy.8), channel_id=1, source_target_pairs={{1,0},{2,1},{3,2},{4,3},{5,4},{6,5},{7,6},{9,8},{10,9},{11,10},{12... | collective-permute-start | bytes 404360 | tf_op jit(solution)/shard_map/ppermute | solution.py:27
  8.5 2.9 %copy.7 = bf16[81,64,13]{0,1,2:T(8,128)(2,1)S(1)} copy(bf16[81,64,13]{2,1,0:T(8,128)(2,1)} %get-tuple-element.132) | data formatting | bytes 269568
  11.4 3.4 %collective-permute-start = (bf16[81,64,13]{0,1,2:T(8,128)(2,1)S(1)}, bf16[81,64,13]{0,1,2:T(8,128)(2,1)S(1)}, u32[]{:S(2)}, u32[]{:S(2)}) collective-permute-start(bf16[81,64,13]{0,1,2:T(8,128)(2,1)S(1)} %copy.7), channel_id=1, source_target_pairs={{0,1},{1,2},{2,3},{3,4},{4,5},{5,6},{6,7},{8,9},{9,10},{10,11},{11... | collective-permute-start | bytes 404360 | tf_op jit(solution)/shard_map/ppermute | solution.py:26
  14.8 5.2 %collective-permute-done = bf16[81,64,13]{0,1,2:T(8,128)(2,1)S(1)} collective-permute-done((bf16[81,64,13]{0,1,2:T(8,128)(2,1)S(1)}, bf16[81,64,13]{0,1,2:T(8,128)(2,1)S(1)}, u32[]{:S(2)}, u32[]{:S(2)}) %collective-permute-start) | collective-permute-done | bytes 134816 | tf_op jit(solution)/shard_map/ppermute | solution.py:26
  20.0 3.2 %copy.5 = bf16[81,64,13]{2,1,0:T(8,128)(2,1)} copy(bf16[81,64,13]{0,1,2:T(8,128)(2,1)S(1)} %collective-permute-done) | data formatting | bytes 269568 | tf_op jit(solution)/shard_map/ppermute | solution.py:26
  23.2 3.2 %copy.6 = bf16[81,64,13]{2,1,0:T(8,128)(2,1)} copy(bf16[81,64,13]{0,1,2:T(8,128)(2,1)S(1)} %collective-permute-done.1) | data formatting | bytes 269568 | tf_op jit(solution)/shard_map/ppermute | solution.py:27
  28.6 2.8 %pad_maximum_fusion = bf16[81,64,282]{2,1,0:T(8,128)(2,1)S(1)} fusion(bf16[81,64,13]{2,1,0:T(8,128)(2,1)S(1)} %copy-done.2, bf16[81,64,256]{2,1,0:T(8,128)(2,1)S(1)} %copy-done, bf16[81,64,13]{2,1,0:T(8,128)(2,1)S(1)} %copy-done.1), kind=kLoop, calls=%fused_computation | loop fusion | flops 8771328 | bytes 5847552 | tf_op jit(solution)/shard_map/concatenate | solution.py:28
  33.3 6.3 %collective-permute-start.4 = (bf16[9,1,282]{2,1,0:T(2,128)(2,1)S(1)}, bf16[9,1,282]{2,1,0:T(2,128)(2,1)S(1)}, u32[]{:S(2)}, u32[]{:S(2)}) collective-permute-start(bf16[9,1,282]{2,1,0:T(2,128)(2,1)S(1)} %get-tuple-element.122), channel_id=1, source_target_pairs={{8,0},{16,8},{24,16},{32,24},{40,32},{48,40},{56,48},{64,56},{72,6... | collective-permute-start | bytes 15236 | tf_op jit(solution)/shard_map/ppermute | solution.py:27
  39.7 2.1 collective-permute-start.8
  41.8 2.2 collective-permute-start.7
  44.0 6.0 %collective-permute-start.9 = (bf16[9,7,282]{2,1,0:T(8,128)(2,1)S(1)}, bf16[9,7,282]{2,1,0:T(8,128)(2,1)S(1)}, u32[]{:S(2)}, u32[]{:S(2)}) collective-permute-start(bf16[9,7,282]{2,1,0:T(8,128)(2,1)S(1)} %get-tuple-element.117), channel_id=1, source_target_pairs={{8,0},{16,8},{24,16},{32,24},{40,32},{48,40},{56,48},{64,56},{72,6... | collective-permute-start | bytes 106604 | tf_op jit(solution)/shard_map/ppermute | solution.py:27
  52.8 6.3 %collective-permute-start.10 = (bf16[9,10,282]{2,1,0:T(8,128)(2,1)S(1)}, bf16[9,10,282]{2,1,0:T(8,128)(2,1)S(1)}, u32[]{:S(2)}, u32[]{:S(2)}) collective-permute-start(bf16[9,10,282]{2,1,0:T(8,128)(2,1)S(1)} %get-tuple-element.115), channel_id=1, source_target_pairs={{8,0},{16,8},{24,16},{32,24},{40,32},{48,40},{56,48},{64,56},{72,6... | collective-permute-start | bytes 152288 | tf_op jit(solution)/shard_map/ppermute | solution.py:27
  61.8 6.3 %collective-permute-start.11 = (bf16[9,13,282]{2,1,0:T(8,128)(2,1)S(1)}, bf16[9,13,282]{2,1,0:T(8,128)(2,1)S(1)}, u32[]{:S(2)}, u32[]{:S(2)}) collective-permute-start(bf16[9,13,282]{2,1,0:T(8,128)(2,1)S(1)} %get-tuple-element.113), channel_id=1, source_target_pairs={{8,0},{16,8},{24,16},{32,24},{40,32},{48,40},{56,48},{64,56},{72,6... | collective-permute-start | bytes 197972 | tf_op jit(solution)/shard_map/ppermute | solution.py:27
  68.3 2.1 collective-permute-start.2
  78.1 27.1 %subtract_multiply_fusion = (f32[64,256]{1,0:T(8,128)}, f32[64,256]{1,0:T(8,128)}, f32[64,256]{1,0:T(8,128)}, f32[64,256]{1,0:T(8,128)}, f32[64,256]{1,0:T(8,128...) fusion(f32[66,282]{1,0:T(8,128)} %get-tuple-element.169, ...), kind=kLoop, calls=%fused_computation.594 | loop fusion | flops 14188544 | bytes 31981568 | tf_op jit(solution)/shard_map/div | solution.py:90
  105.2 7.2 %fusion.344 = (f32[64,256]{1,0:T(8,128)S(1)}, f32[64,256]{1,0:T(8,128)S(1)}, f32[64,256]{1,0:T(8,128)S(1)}) fusion(f32[64,256]{1,0:T(8,128)} %get-tuple-element.31, f32[65,256]{1,0:T(8,128)S(1)} %fusion.3, f32[64,257]{1,0:T(8,128)S(1)} %fusion.1, f32[64,256]{1,0:T(8,128)} %get-tuple-element.112, f32[66,282]{1,0:T(8,128)} %get-tuple-element.134, ...), kind=kLoop, calls=%fused_computation.859 | loop fusion | flops 8077312 | bytes 11206656 | tf_op jit(solution)/shard_map/div | solution.py:106
  112.5 4.6 %collective-permute-start.13 = (f32[1,256]{1,0:T(1,128)S(1)}, f32[1,256]{1,0:T(1,128)S(1)}, u32[]{:S(2)}, u32[]{:S(2)}) collective-permute-start(f32[1,256]{1,0:T(1,128)S(1)} %get-tuple-element.221), channel_id=1, source_target_pairs={{8,0},{16,8},{24,16},{32,24},{40,32},{48,40},{56,48},{64,56},{72,6... | collective-permute-start | bytes 3080 | tf_op jit(solution)/shard_map/ppermute | solution.py:27
  119.0 5.6 %collective-permute-done.12 = f32[1,256]{1,0:T(1,128)S(1)} collective-permute-done((f32[1,256]{1,0:T(1,128)S(1)}, f32[1,256]{1,0:T(1,128)S(1)}, u32[]{:S(2)}, u32[]{:S(2)}) %collective-permute-start.12) | collective-permute-done | bytes 1056 | tf_op jit(solution)/shard_map/ppermute | solution.py:26
  126.7 3.9 %collective-permute-start.15 = (f32[66,1]{1,0:T(8,128)S(1)}, f32[66,1]{1,0:T(8,128)S(1)}, u32[]{:S(2)}, u32[]{:S(2)}) collective-permute-start(f32[66,1]{1,0:T(8,128)S(1)} %get-tuple-element.218), channel_id=1, source_target_pairs={{0,1},{1,2},{2,3},{3,4},{4,5},{5,6},{6,7},{8,9},{9,10},{10,11},{11... | collective-permute-start | bytes 800 | tf_op jit(solution)/shard_map/ppermute | solution.py:26
  135.2 2.4 collective-permute-start.16
  137.6 9.3 %all-reduce.5 = (f32[]{:T(128)}, f32[]{:T(128)}) all-reduce(f32[]{:T(128)} %get-tuple-element.5, f32[]{:T(128)} %get-tuple-element.4), channel_id=1, replica_groups=mesh['row_0'=4,'row_1'=4,'row_2'=2,'col_0'=2,'col_1'=4] {'row_0'}, use_global_device_ids=true, to_apply=%region_1.2 | all-reduce | flops 2 | bytes 16 | tf_op jit(solution)/shard_map/psum | solution.py:34
  146.9 9.0 %all-reduce.3 = (f32[]{:T(128)}, f32[]{:T(128)}) all-reduce(f32[]{:T(128)} %get-tuple-element.16, f32[]{:T(128)} %get-tuple-element.17), channel_id=1, replica_groups=mesh['row_0'=4,'row_1'=4,'row_2'=2,'col_0'=2,'col_1'=4] {'row_1'}, use_global_device_ids=true, to_apply=%region_2.3 | all-reduce | flops 2 | bytes 16 | tf_op jit(solution)/shard_map/psum | solution.py:34
  155.9 3.2 %all-reduce.9 = (f32[]{:T(128)}, f32[]{:T(128)}) all-reduce(f32[]{:T(128)} %get-tuple-element.12, f32[]{:T(128)} %get-tuple-element.13), channel_id=1, replica_groups=mesh['row_0'=4,'row_1'=4,'row_2'=2,'col_0'=2,'col_1'=4] {'row_2'}, use_global_device_ids=true, to_apply=%region_3.4 | all-reduce | flops 2 | bytes 16 | tf_op jit(solution)/shard_map/psum | solution.py:34
  159.2 17.8 %all-reduce.7 = (f32[]{:T(128)}, f32[]{:T(128)}) all-reduce(f32[]{:T(128)} %get-tuple-element.24, f32[]{:T(128)} %get-tuple-element.25), channel_id=1, replica_groups=mesh['row_0'=4,'row_1'=4,'row_2'=2,'col_0'=2,'col_1'=4] {'col_0'}, use_global_device_ids=true, to_apply=%region_4.5 | all-reduce | flops 2 | bytes 16 | tf_op jit(solution)/shard_map/psum | solution.py:34
  177.0 7.9 %collective-permute-start.18 = (f32[66,1]{1,0:T(8,128)S(1)}, f32[66,1]{1,0:T(8,128)S(1)}, u32[]{:S(2)}, u32[]{:S(2)}) collective-permute-start(f32[66,1]{1,0:T(8,128)S(1)} %get-tuple-element.215), channel_id=1, source_target_pairs={{1,0},{2,1},{3,2},{4,3},{5,4},{6,5},{7,6},{9,8},{10,9},{11,10},{12... | collective-permute-start | bytes 800 | tf_op jit(solution)/shard_map/ppermute | solution.py:27
  186.9 13.7 %all-reduce.1 = (f32[]{:T(128)}, f32[]{:T(128)}) all-reduce(f32[]{:T(128)} %get-tuple-element.20, f32[]{:T(128)} %get-tuple-element.21), channel_id=1, replica_groups=mesh['row_0'=4,'row_1'=4,'row_2'=2,'col_0'=2,'col_1'=4] {'col_1'}, use_global_device_ids=true, to_apply=%region_5.6 | all-reduce | flops 2 | bytes 16 | tf_op jit(solution)/shard_map/psum | solution.py:34
  203.7 11.0 %all-reduce.4 = (f32[]{:T(128)}, f32[]{:T(128)}) all-reduce(f32[]{:T(128)} %get-tuple-element.3, f32[]{:T(128)} %get-tuple-element.2), channel_id=1, replica_groups=mesh['row_0'=4,'row_1'=4,'row_2'=2,'col_0'=2,'col_1'=4] {'row_0'}, use_global_device_ids=true, to_apply=%region_13.14 | all-reduce | flops 2 | bytes 16 | tf_op jit(solution)/shard_map/psum | solution.py:34
  214.8 11.0 %all-reduce.2 = (f32[]{:T(128)}, f32[]{:T(128)}) all-reduce(f32[]{:T(128)} %get-tuple-element.14, f32[]{:T(128)} %get-tuple-element.15), channel_id=1, replica_groups=mesh['row_0'=4,'row_1'=4,'row_2'=2,'col_0'=2,'col_1'=4] {'row_1'}, use_global_device_ids=true, to_apply=%region_14.15 | all-reduce | flops 2 | bytes 16 | tf_op jit(solution)/shard_map/psum | solution.py:34
  225.8 3.1 %all-reduce.8 = (f32[]{:T(128)}, f32[]{:T(128)}) all-reduce(f32[]{:T(128)} %get-tuple-element.10, f32[]{:T(128)} %get-tuple-element.11), channel_id=1, replica_groups=mesh['row_0'=4,'row_1'=4,'row_2'=2,'col_0'=2,'col_1'=4] {'row_2'}, use_global_device_ids=true, to_apply=%region_15.16 | all-reduce | flops 2 | bytes 16 | tf_op jit(solution)/shard_map/psum | solution.py:34
  228.9 9.5 %all-reduce.6 = (f32[]{:T(128)}, f32[]{:T(128)}) all-reduce(f32[]{:T(128)} %get-tuple-element.22, f32[]{:T(128)} %get-tuple-element.23), channel_id=1, replica_groups=mesh['row_0'=4,'row_1'=4,'row_2'=2,'col_0'=2,'col_1'=4] {'col_0'}, use_global_device_ids=true, to_apply=%region_16.17 | all-reduce | flops 2 | bytes 16 | tf_op jit(solution)/shard_map/psum | solution.py:34
  238.3 11.6 %all-reduce = (f32[]{:T(128)}, f32[]{:T(128)}) all-reduce(f32[]{:T(128)} %get-tuple-element.18, f32[]{:T(128)} %get-tuple-element.19), channel_id=1, replica_groups=mesh['row_0'=4,'row_1'=4,'row_2'=2,'col_0'=2,'col_1'=4] {'col_1'}, use_global_device_ids=true, to_apply=%region_17.18 | all-reduce | flops 2 | bytes 16 | tf_op jit(solution)/shard_map/psum | solution.py:34
  (67 shorter events, 32.7 us)
Async XLA Ops:
  5.8 20.6 %copy-start = (bf16[81,64,256]{2,1,0:T(8,128)(2,1)S(1)}, bf16[81,64,256]{2,1,0:T(8,128)(2,1)}, u32[]{:S(2)}) copy-start(bf16[81,64,256]{2,1,0:T(8,128)(2,1)} %param.1) | copy-start | bytes 7962628
  5.8 17.4 %collective-permute-start.1 = (bf16[81,64,13]{0,1,2:T(8,128)(2,1)S(1)}, bf16[81,64,13]{0,1,2:T(8,128)(2,1)S(1)}, u32[]{:S(2)}, u32[]{:S(2)}) collective-permute-start(bf16[81,64,13]{0,1,2:T(8,128)(2,1)S(1)} %copy.8), channel_id=1, source_target_pairs={{1,0},{2,1},{3,2},{4,3},{5,4},{6,5},{7,6},{9,8},{10,9},{11,10},{12... | collective-permute-start | bytes 404360 | tf_op jit(solution)/shard_map/ppermute | solution.py:27
  11.4 8.6 %collective-permute-start = (bf16[81,64,13]{0,1,2:T(8,128)(2,1)S(1)}, bf16[81,64,13]{0,1,2:T(8,128)(2,1)S(1)}, u32[]{:S(2)}, u32[]{:S(2)}) collective-permute-start(bf16[81,64,13]{0,1,2:T(8,128)(2,1)S(1)} %copy.7), channel_id=1, source_target_pairs={{0,1},{1,2},{2,3},{3,4},{4,5},{5,6},{6,7},{8,9},{9,10},{10,11},{11... | collective-permute-start | bytes 404360 | tf_op jit(solution)/shard_map/ppermute | solution.py:26
  26.4 1.4 copy-start.1
  26.4 1.8 copy-start.2
  31.4 19.5 %collective-permute-start.3 = (bf16[9,1,282]{2,1,0:T(2,128)(2,1)S(1)}, bf16[9,1,282]{2,1,0:T(2,128)(2,1)S(1)}, u32[]{:S(2)}, u32[]{:S(2)}) collective-permute-start(bf16[9,1,282]{2,1,0:T(2,128)(2,1)S(1)} %get-tuple-element.121), channel_id=1, source_target_pairs={{0,8},{8,16},{16,24},{24,32},{32,40},{40,48},{48,56},{56,64},{64,7... | collective-permute-start | bytes 15236 | tf_op jit(solution)/shard_map/ppermute | solution.py:26
  33.3 19.5 %collective-permute-start.4 = (bf16[9,1,282]{2,1,0:T(2,128)(2,1)S(1)}, bf16[9,1,282]{2,1,0:T(2,128)(2,1)S(1)}, u32[]{:S(2)}, u32[]{:S(2)}) collective-permute-start(bf16[9,1,282]{2,1,0:T(2,128)(2,1)S(1)} %get-tuple-element.122), channel_id=1, source_target_pairs={{8,0},{16,8},{24,16},{32,24},{40,32},{48,40},{56,48},{64,56},{72,6... | collective-permute-start | bytes 15236 | tf_op jit(solution)/shard_map/ppermute | solution.py:27
  39.7 20.1 %collective-permute-start.8 = (bf16[9,4,282]{2,1,0:T(4,128)(2,1)S(1)}, bf16[9,4,282]{2,1,0:T(4,128)(2,1)S(1)}, u32[]{:S(2)}, u32[]{:S(2)}) collective-permute-start(bf16[9,4,282]{2,1,0:T(4,128)(2,1)S(1)} %get-tuple-element.119), channel_id=1, source_target_pairs={{8,0},{16,8},{24,16},{32,24},{40,32},{48,40},{56,48},{64,56},{72,6... | collective-permute-start | bytes 60920 | tf_op jit(solution)/shard_map/ppermute | solution.py:27
  41.8 20.0 %collective-permute-start.7 = (bf16[9,4,282]{2,1,0:T(4,128)(2,1)S(1)}, bf16[9,4,282]{2,1,0:T(4,128)(2,1)S(1)}, u32[]{:S(2)}, u32[]{:S(2)}) collective-permute-start(bf16[9,4,282]{2,1,0:T(4,128)(2,1)S(1)} %get-tuple-element.120), channel_id=1, source_target_pairs={{0,8},{8,16},{16,24},{24,32},{32,40},{40,48},{48,56},{56,64},{64,7... | collective-permute-start | bytes 60920 | tf_op jit(solution)/shard_map/ppermute | solution.py:26
  44.0 27.3 %collective-permute-start.9 = (bf16[9,7,282]{2,1,0:T(8,128)(2,1)S(1)}, bf16[9,7,282]{2,1,0:T(8,128)(2,1)S(1)}, u32[]{:S(2)}, u32[]{:S(2)}) collective-permute-start(bf16[9,7,282]{2,1,0:T(8,128)(2,1)S(1)} %get-tuple-element.117), channel_id=1, source_target_pairs={{8,0},{16,8},{24,16},{32,24},{40,32},{48,40},{56,48},{64,56},{72,6... | collective-permute-start | bytes 106604 | tf_op jit(solution)/shard_map/ppermute | solution.py:27
  50.9 17.4 %collective-permute-start.6 = (bf16[9,7,282]{2,1,0:T(8,128)(2,1)S(1)}, bf16[9,7,282]{2,1,0:T(8,128)(2,1)S(1)}, u32[]{:S(2)}, u32[]{:S(2)}) collective-permute-start(bf16[9,7,282]{2,1,0:T(8,128)(2,1)S(1)} %get-tuple-element.118), channel_id=1, source_target_pairs={{0,8},{8,16},{16,24},{24,32},{32,40},{40,48},{48,56},{56,64},{64,7... | collective-permute-start | bytes 106604 | tf_op jit(solution)/shard_map/ppermute | solution.py:26
  52.8 20.5 %collective-permute-start.10 = (bf16[9,10,282]{2,1,0:T(8,128)(2,1)S(1)}, bf16[9,10,282]{2,1,0:T(8,128)(2,1)S(1)}, u32[]{:S(2)}, u32[]{:S(2)}) collective-permute-start(bf16[9,10,282]{2,1,0:T(8,128)(2,1)S(1)} %get-tuple-element.115), channel_id=1, source_target_pairs={{8,0},{16,8},{24,16},{32,24},{40,32},{48,40},{56,48},{64,56},{72,6... | collective-permute-start | bytes 152288 | tf_op jit(solution)/shard_map/ppermute | solution.py:27
  59.7 12.6 %collective-permute-start.5 = (bf16[9,10,282]{2,1,0:T(8,128)(2,1)S(1)}, bf16[9,10,282]{2,1,0:T(8,128)(2,1)S(1)}, u32[]{:S(2)}, u32[]{:S(2)}) collective-permute-start(bf16[9,10,282]{2,1,0:T(8,128)(2,1)S(1)} %get-tuple-element.116), channel_id=1, source_target_pairs={{0,8},{8,16},{16,24},{24,32},{32,40},{40,48},{48,56},{56,64},{64,7... | collective-permute-start | bytes 152288 | tf_op jit(solution)/shard_map/ppermute | solution.py:26
  61.8 12.5 %collective-permute-start.11 = (bf16[9,13,282]{2,1,0:T(8,128)(2,1)S(1)}, bf16[9,13,282]{2,1,0:T(8,128)(2,1)S(1)}, u32[]{:S(2)}, u32[]{:S(2)}) collective-permute-start(bf16[9,13,282]{2,1,0:T(8,128)(2,1)S(1)} %get-tuple-element.113), channel_id=1, source_target_pairs={{8,0},{16,8},{24,16},{32,24},{40,32},{48,40},{56,48},{64,56},{72,6... | collective-permute-start | bytes 197972 | tf_op jit(solution)/shard_map/ppermute | solution.py:27
  68.3 8.8 %collective-permute-start.2 = (bf16[9,13,282]{2,1,0:T(8,128)(2,1)S(1)}, bf16[9,13,282]{2,1,0:T(8,128)(2,1)S(1)}, u32[]{:S(2)}, u32[]{:S(2)}) collective-permute-start(bf16[9,13,282]{2,1,0:T(8,128)(2,1)S(1)} %get-tuple-element.114), channel_id=1, source_target_pairs={{0,8},{8,16},{16,24},{24,32},{32,40},{40,48},{48,56},{56,64},{64,7... | collective-permute-start | bytes 197972 | tf_op jit(solution)/shard_map/ppermute | solution.py:26
  105.2 27.3 %copy-start.3 = (f32[64,256]{1,0:T(8,128)S(1)}, f32[64,256]{1,0:T(8,128)}, u32[]{:S(2)}) copy-start(f32[64,256]{1,0:T(8,128)} %get-tuple-element.31) | copy-start | bytes 196612
  112.4 20.8 %copy-start.4 = (f32[64,256]{1,0:T(8,128)}, f32[64,256]{1,0:T(8,128)S(1)}, u32[]{:S(2)}) copy-start(f32[64,256]{1,0:T(8,128)S(1)} %get-tuple-element.30) | copy-start | bytes 196612
  112.5 6.5 %collective-permute-start.13 = (f32[1,256]{1,0:T(1,128)S(1)}, f32[1,256]{1,0:T(1,128)S(1)}, u32[]{:S(2)}, u32[]{:S(2)}) collective-permute-start(f32[1,256]{1,0:T(1,128)S(1)} %get-tuple-element.221), channel_id=1, source_target_pairs={{8,0},{16,8},{24,16},{32,24},{40,32},{48,40},{56,48},{64,56},{72,6... | collective-permute-start | bytes 3080 | tf_op jit(solution)/shard_map/ppermute | solution.py:27
  117.1 7.6 %collective-permute-start.12 = (f32[1,256]{1,0:T(1,128)S(1)}, f32[1,256]{1,0:T(1,128)S(1)}, u32[]{:S(2)}, u32[]{:S(2)}) collective-permute-start(f32[1,256]{1,0:T(1,128)S(1)} %get-tuple-element.222), channel_id=1, source_target_pairs={{0,8},{8,16},{16,24},{24,32},{32,40},{40,48},{48,56},{56,64},{64,7... | collective-permute-start | bytes 3080 | tf_op jit(solution)/shard_map/ppermute | solution.py:26
  124.7 5.9 %collective-permute-start.14 = (f32[66,1]{1,0:T(8,128)S(1)}, f32[66,1]{1,0:T(8,128)S(1)}, u32[]{:S(2)}, u32[]{:S(2)}) collective-permute-start(f32[66,1]{1,0:T(8,128)S(1)} %get-tuple-element.217), channel_id=1, source_target_pairs={{1,0},{2,1},{3,2},{4,3},{5,4},{6,5},{7,6},{9,8},{10,9},{11,10},{12... | collective-permute-start | bytes 800 | tf_op jit(solution)/shard_map/ppermute | solution.py:27
  126.7 5.9 %collective-permute-start.15 = (f32[66,1]{1,0:T(8,128)S(1)}, f32[66,1]{1,0:T(8,128)S(1)}, u32[]{:S(2)}, u32[]{:S(2)}) collective-permute-start(f32[66,1]{1,0:T(8,128)S(1)} %get-tuple-element.218), channel_id=1, source_target_pairs={{0,1},{1,2},{2,3},{3,4},{4,5},{5,6},{6,7},{8,9},{9,10},{10,11},{11... | collective-permute-start | bytes 800 | tf_op jit(solution)/shard_map/ppermute | solution.py:26
  133.3 43.6 %collective-permute-start.17 = (f32[1,256]{1,0:T(1,128)S(1)}, f32[1,256]{1,0:T(1,128)S(1)}, u32[]{:S(2)}, u32[]{:S(2)}) collective-permute-start(f32[1,256]{1,0:T(1,128)S(1)} %get-tuple-element.219), channel_id=1, source_target_pairs={{8,0},{16,8},{24,16},{32,24},{40,32},{48,40},{56,48},{64,56},{72,6... | collective-permute-start | bytes 3080 | tf_op jit(solution)/shard_map/ppermute | solution.py:27
  135.2 41.7 %collective-permute-start.16 = (f32[1,256]{1,0:T(1,128)S(1)}, f32[1,256]{1,0:T(1,128)S(1)}, u32[]{:S(2)}, u32[]{:S(2)}) collective-permute-start(f32[1,256]{1,0:T(1,128)S(1)} %get-tuple-element.220), channel_id=1, source_target_pairs={{0,8},{8,16},{16,24},{24,32},{32,40},{40,48},{48,56},{56,64},{64,7... | collective-permute-start | bytes 3080 | tf_op jit(solution)/shard_map/ppermute | solution.py:26
  177.0 25.0 %collective-permute-start.18 = (f32[66,1]{1,0:T(8,128)S(1)}, f32[66,1]{1,0:T(8,128)S(1)}, u32[]{:S(2)}, u32[]{:S(2)}) collective-permute-start(f32[66,1]{1,0:T(8,128)S(1)} %get-tuple-element.215), channel_id=1, source_target_pairs={{1,0},{2,1},{3,2},{4,3},{5,4},{6,5},{7,6},{9,8},{10,9},{11,10},{12... | collective-permute-start | bytes 800 | tf_op jit(solution)/shard_map/ppermute | solution.py:27
  185.0 17.1 %collective-permute-start.19 = (f32[66,1]{1,0:T(8,128)S(1)}, f32[66,1]{1,0:T(8,128)S(1)}, u32[]{:S(2)}, u32[]{:S(2)}) collective-permute-start(f32[66,1]{1,0:T(8,128)S(1)} %get-tuple-element.216), channel_id=1, source_target_pairs={{0,1},{1,2},{2,3},{3,4},{4,5},{5,6},{6,7},{8,9},{9,10},{10,11},{11... | collective-permute-start | bytes 800 | tf_op jit(solution)/shard_map/ppermute | solution.py:26
where the time goes:
time: 257 us; the launch traced here: 256 us
  blocking collectives  99.2 us (39%)
  starting transfers between devices  69.9 us (27%)
  other arithmetic  49.4 us (19%)
  local copies, waits for them, and re-layouts  16 us (6%)
  waiting for transfers between devices  14.5 us (6%)
  between operations  7.14 us (3%)
    psum x10, blocking collectives, by_axis(): array = lax.psum(array, axis)  99.2 us
    ppermute x10, starting transfers between devices, with_halo(): after = lax.ppermute(leading, axis, down)  46.2 us
    div x1, other arithmetic, shards(): source = source_sum / VIEWS  27.1 us
    ppermute x10, starting transfers between devices, with_halo(): before = lax.ppermute(last, axis, up)  23.7 us
    ppermute x10, waiting for transfers between devices, with_halo(): before = lax.ppermute(last, axis, up)  14.5 us
    div x1, other arithmetic, shards(): scaled_res = residual / precond  7.21 us
    convert_element_type x9, other arithmetic, shards(): image = band[tindex].astype(jnp.float32)  6.21 us
    unnamed x12, local copies, waits for them, and re-layouts  5.38 us
  transfers between devices with their start and end apart: 20, of which 4 were waited for; matrix products, arithmetic and copies ran while one was open for 5% of the time, Pallas kernels for 0%

commit v1 on v0

--- a/solution.py
+++ b/solution.py
@@ -31,7 +31,7 @@
 
 def by_axis(array, axes):
     for axis in axes:
-        array = lax.psum(array, axis)
+        array = jnp.sum(jax.lax.all_gather(array, axis), axis=0)
     return array
 
 

time: 257 us -> 293 us (1.14)
  local copies, waits for them, and re-layouts: 16 us -> 48.8 us
  other arithmetic: 49.4 us -> 64.8 us
  starting transfers between devices: 69.9 us -> 61.7 us
  waiting for transfers between devices: 14.5 us -> 6.51 us
    unnamed x0 -> x10, blocking collectives: none -> 101 us
    psum x10 -> x0, blocking collectives: 99.2 us -> none  [by_axis(): array = lax.psum(array, axis)]
    unnamed x12 -> x53, local copies, waits for them, and re-layouts: 5.38 us -> 38.3 us
    ppermute x10, starting transfers between devices: 46.2 us -> 33.6 us  [with_halo(): after = lax.ppermute(leading, axis, down)]
    reduce_sum x0 -> x20, other arithmetic: none -> 12.5 us  [by_axis(): array = jnp.sum(jax.lax.all_gather(array, axis), axis=0)]
    ppermute x10, waiting for transfers between devices: 14.5 us -> 3.71 us  [with_halo(): before = lax.ppermute(last, axis, up)]
    ppermute x10, starting transfers between devices: 23.7 us -> 28.1 us  [with_halo(): before = lax.ppermute(last, axis, up)]
  transfers between devices with their start and end apart: 20 -> 20, of which waited for: 4 -> 5; matrix products, arithmetic and copies ran while one was open for 5% -> 11% of each run, Pallas kernels for 0% -> 0%
where the time goes in v1:
time: 293 us; the launch traced here: 290 us
  blocking collectives  101 us (34%)
  other arithmetic  64.8 us (22%)
  starting transfers between devices  61.7 us (21%)
  local copies, waits for them, and re-layouts  48.8 us (17%)
  between operations  7.15 us (2%)
  waiting for transfers between devices  6.51 us (2%)
    unnamed x10, blocking collectives  101 us
    unnamed x53, local copies, waits for them, and re-layouts  38.3 us
    ppermute x10, starting transfers between devices, with_halo(): after = lax.ppermute(leading, axis, down)  33.6 us
    ppermute x10, starting transfers between devices, with_halo(): before = lax.ppermute(last, axis, up)  28.1 us
    div x1, other arithmetic, shards(): source = source_sum / VIEWS  27 us
    reduce_sum x20, other arithmetic, by_axis(): array = jnp.sum(jax.lax.all_gather(array, axis), axis=0)  12.5 us
    div x1, other arithmetic, shards(): scaled_res = residual / precond  7.86 us
    convert_element_type x9, other arithmetic, shards(): image = band[tindex].astype(jnp.float32)  6.25 us
  transfers between devices with their start and end apart: 20, of which 5 were waited for; matrix products, arithmetic and copies ran while one was open for 11% of the time, Pallas kernels for 0%

profile of v1, /device:TPU:10, one launch (start us, length us, event | category | flops | bytes accessed | tf_op | source)
XLA Modules:
  0.0 289.8 jit_solution(322235027046883568)
XLA Ops:
  0.6 3.4 %fusion.427 = (bf16[81,64,13]{2,1,0:T(8,128)(2,1)S(1)}, bf16[81,64,13]{2,1,0:T(8,128)(2,1)}) fusion(bf16[81,64,256]{2,1,0:T(8,128)(2,1)} %param.1), kind=kLoop, calls=%fused_computation.861 | loop fusion | bytes 539136 | tf_op jit(solution)/shard_map/slice | solution.py:24
  5.8 3.7 %collective-permute-start = (bf16[81,64,13]{0,1,2:T(8,128)(2,1)S(1)}, bf16[81,64,13]{0,1,2:T(8,128)(2,1)S(1)}, u32[]{:S(2)}, u32[]{:S(2)}) collective-permute-start(bf16[81,64,13]{0,1,2:T(8,128)(2,1)S(1)} %copy.7), channel_id=1, source_target_pairs={{0,1},{1,2},{2,3},{3,4},{4,5},{5,6},{6,7},{8,9},{9,10},{10,11},{11... | collective-permute-start | bytes 404360 | tf_op jit(solution)/shard_map/ppermute | solution.py:26
  9.4 2.9 copy.8
  12.3 2.5 collective-permute-start.1
  14.9 3.2 %copy.5 = bf16[81,64,13]{2,1,0:T(8,128)(2,1)} copy(bf16[81,64,13]{0,1,2:T(8,128)(2,1)S(1)} %collective-permute-done) | data formatting | bytes 269568 | tf_op jit(solution)/shard_map/ppermute | solution.py:26
  18.1 2.8 collective-permute-done.1
  20.9 3.2 %copy.6 = bf16[81,64,13]{2,1,0:T(8,128)(2,1)} copy(bf16[81,64,13]{0,1,2:T(8,128)(2,1)S(1)} %collective-permute-done.1) | data formatting | bytes 269568 | tf_op jit(solution)/shard_map/ppermute | solution.py:27
  24.1 4.3 %pad_maximum_fusion = bf16[81,64,282]{2,1,0:T(8,128)(2,1)S(1)} fusion(bf16[81,64,13]{2,1,0:T(8,128)(2,1)} %copy.6, bf16[81,64,256]{2,1,0:T(8,128)(2,1)S(1)} %copy-done, bf16[81,64,13]{2,1,0:T(8,128)(2,1)} %copy.5), kind=kLoop, calls=%fused_computation | loop fusion | flops 8771328 | bytes 5847552 | tf_op jit(solution)/shard_map/concatenate | solution.py:28
  31.5 6.3 %collective-permute-start.4 = (bf16[9,1,282]{2,1,0:T(2,128)(2,1)S(1)}, bf16[9,1,282]{2,1,0:T(2,128)(2,1)S(1)}, u32[]{:S(2)}, u32[]{:S(2)}) collective-permute-start(bf16[9,1,282]{2,1,0:T(2,128)(2,1)S(1)} %get-tuple-element.122), channel_id=1, source_target_pairs={{8,0},{16,8},{24,16},{32,24},{40,32},{48,40},{56,48},{64,56},{72,6... | collective-permute-start | bytes 15236 | tf_op jit(solution)/shard_map/ppermute | solution.py:27
  37.9 2.1 collective-permute-start.11
  40.0 3.6 %collective-permute-start.10 = (bf16[9,10,282]{2,1,0:T(8,128)(2,1)S(1)}, bf16[9,10,282]{2,1,0:T(8,128)(2,1)S(1)}, u32[]{:S(2)}, u32[]{:S(2)}) collective-permute-start(bf16[9,10,282]{2,1,0:T(8,128)(2,1)S(1)} %get-tuple-element.115), channel_id=1, source_target_pairs={{8,0},{16,8},{24,16},{32,24},{40,32},{48,40},{56,48},{64,56},{72,6... | collective-permute-start | bytes 152288 | tf_op jit(solution)/shard_map/ppermute | solution.py:27
  45.6 2.1 collective-permute-start.8
  47.8 2.2 collective-permute-start.7
  50.6 3.6 %collective-permute-start.6 = (bf16[9,7,282]{2,1,0:T(8,128)(2,1)S(1)}, bf16[9,7,282]{2,1,0:T(8,128)(2,1)S(1)}, u32[]{:S(2)}, u32[]{:S(2)}) collective-permute-start(bf16[9,7,282]{2,1,0:T(8,128)(2,1)S(1)} %get-tuple-element.118), channel_id=1, source_target_pairs={{0,8},{8,16},{16,24},{24,32},{32,40},{40,48},{48,56},{56,64},{64,7... | collective-permute-start | bytes 106604 | tf_op jit(solution)/shard_map/ppermute | solution.py:26
  67.4 27.0 %subtract_multiply_fusion = (f32[64,256]{1,0:T(8,128)}, f32[64,256]{1,0:T(8,128)}, f32[64,256]{1,0:T(8,128)}, f32[64,256]{1,0:T(8,128)}, f32[64,256]{1,0:T(8,128...) fusion(f32[66,282]{1,0:T(8,128)} %get-tuple-element.169, ...), kind=kLoop, calls=%fused_computation.594 | loop fusion | flops 14188544 | bytes 31981568 | tf_op jit(solution)/shard_map/div | solution.py:90
  94.4 7.9 %fusion.344 = (f32[64,256]{1,0:T(8,128)S(1)}, f32[64,256]{1,0:T(8,128)}, f32[64,256]{1,0:T(8,128)}) fusion(f32[64,256]{1,0:T(8,128)} %get-tuple-element.31, f32[65,256]{1,0:T(8,128)S(1)} %fusion.3, f32[64,257]{1,0:T(8,128)S(1)} %fusion.1, f32[64,256]{1,0:T(8,128)} %get-tuple-element.112, f32[66,282]{1,0:T(8,128)} %get-tuple-element.134, ...), kind=kLoop, calls=%fused_computation.859 | loop fusion | flops 8077312 | bytes 11206656 | tf_op jit(solution)/shard_map/div | solution.py:106
  104.2 6.3 %collective-permute-start.13 = (f32[1,256]{1,0:T(1,128)S(1)}, f32[1,256]{1,0:T(1,128)S(1)}, u32[]{:S(2)}, u32[]{:S(2)}) collective-permute-start(f32[1,256]{1,0:T(1,128)S(1)} %get-tuple-element.221), channel_id=1, source_target_pairs={{8,0},{16,8},{24,16},{32,24},{40,32},{48,40},{56,48},{64,56},{72,6... | collective-permute-start | bytes 3080 | tf_op jit(solution)/shard_map/ppermute | solution.py:27
  113.2 2.4 collective-permute-start.14
  115.7 6.1 %collective-permute-start.15 = (f32[66,1]{1,0:T(8,128)S(1)}, f32[66,1]{1,0:T(8,128)S(1)}, u32[]{:S(2)}, u32[]{:S(2)}) collective-permute-start(f32[66,1]{1,0:T(8,128)S(1)} %get-tuple-element.218), channel_id=1, source_target_pairs={{0,1},{1,2},{2,3},{3,4},{4,5},{5,6},{6,7},{8,9},{9,10},{10,11},{11... | collective-permute-start | bytes 800 | tf_op jit(solution)/shard_map/ppermute | solution.py:26
  129.7 8.7 %all-reduce.25 = (f32[4]{0:T(128)S(1)}, f32[4]{0:T(128)S(1)}) all-reduce(f32[4]{0:T(128)S(1)} %dynamic-update-slice, f32[4]{0:T(128)S(1)} %dynamic-update-slice.5), channel_id=1, replica_groups=mesh['row_0'=4,'row_1'=4,'row_2'=2,'col_0'=2,'col_1'=4] {'row_0'}, use_global_device_ids=true, to_apply=%add | all-reduce | flops 8 | bytes 64
  144.3 9.6 %all-reduce.23 = (f32[4]{0:T(128)S(1)}, f32[4]{0:T(128)S(1)}) all-reduce(f32[4]{0:T(128)S(1)} %dynamic-update-slice.1, f32[4]{0:T(128)S(1)} %dynamic-update-slice.6), channel_id=1, replica_groups=mesh['row_0'=4,'row_1'=4,'row_2'=2,'col_0'=2,'col_1'=4] {'row_1'}, use_global_device_ids=true, to_apply=%add.1 | all-reduce | flops 8 | bytes 64
  157.8 3.1 %collective-permute-start.17 = (f32[1,256]{1,0:T(1,128)S(1)}, f32[1,256]{1,0:T(1,128)S(1)}, u32[]{:S(2)}, u32[]{:S(2)}) collective-permute-start(f32[1,256]{1,0:T(1,128)S(1)} %get-tuple-element.219), channel_id=1, source_target_pairs={{8,0},{16,8},{24,16},{32,24},{40,32},{48,40},{56,48},{64,56},{72,6... | collective-permute-start | bytes 3080 | tf_op jit(solution)/shard_map/ppermute | solution.py:27
  160.9 2.6 all-reduce.29
  168.9 20.6 %all-reduce.27 = (f32[2]{0:T(128)S(1)}, f32[2]{0:T(128)S(1)}) all-reduce(f32[2]{0:T(128)S(1)} %dynamic-update-slice.3, f32[2]{0:T(128)S(1)} %dynamic-update-slice.8), channel_id=1, replica_groups=mesh['row_0'=4,'row_1'=4,'row_2'=2,'col_0'=2,'col_1'=4] {'col_0'}, use_global_device_ids=true, to_apply=%add.3 | all-reduce | flops 4 | bytes 32
  193.5 15.7 %all-reduce.21 = (f32[4]{0:T(128)S(1)}, f32[4]{0:T(128)S(1)}) all-reduce(f32[4]{0:T(128)S(1)} %dynamic-update-slice.4, f32[4]{0:T(128)S(1)} %dynamic-update-slice.9), channel_id=1, replica_groups=mesh['row_0'=4,'row_1'=4,'row_2'=2,'col_0'=2,'col_1'=4] {'col_1'}, use_global_device_ids=true, to_apply=%add.4 | all-reduce | flops 8 | bytes 64
  209.4 3.2 %collective-permute-start.18 = (f32[66,1]{1,0:T(8,128)S(1)}, f32[66,1]{1,0:T(8,128)S(1)}, u32[]{:S(2)}, u32[]{:S(2)}) collective-permute-start(f32[66,1]{1,0:T(8,128)S(1)} %get-tuple-element.215), channel_id=1, source_target_pairs={{1,0},{2,1},{3,2},{4,3},{5,4},{6,5},{7,6},{9,8},{10,9},{11,10},{12... | collective-permute-start | bytes 800 | tf_op jit(solution)/shard_map/ppermute | solution.py:27
  212.5 2.7 collective-permute-start.19
  222.8 8.5 %all-reduce.24 = (f32[4]{0:T(128)S(1)}, f32[4]{0:T(128)S(1)}) all-reduce(f32[4]{0:T(128)S(1)} %dynamic-update-slice.10, f32[4]{0:T(128)S(1)} %dynamic-update-slice.15), channel_id=1, replica_groups=mesh['row_0'=4,'row_1'=4,'row_2'=2,'col_0'=2,'col_1'=4] {'row_0'}, use_global_device_ids=true, to_apply=%add.10 | all-reduce | flops 8 | bytes 64
  235.2 9.9 %all-reduce.22 = (f32[4]{0:T(128)S(1)}, f32[4]{0:T(128)S(1)}) all-reduce(f32[4]{0:T(128)S(1)} %dynamic-update-slice.11, f32[4]{0:T(128)S(1)} %dynamic-update-slice.16), channel_id=1, replica_groups=mesh['row_0'=4,'row_1'=4,'row_2'=2,'col_0'=2,'col_1'=4] {'row_1'}, use_global_device_ids=true, to_apply=%add.11 | all-reduce | flops 8 | bytes 64
  248.9 2.4 all-reduce.28
  255.3 8.8 %all-reduce.26 = (f32[2]{0:T(128)S(1)}, f32[2]{0:T(128)S(1)}) all-reduce(f32[2]{0:T(128)S(1)} %dynamic-update-slice.13, f32[2]{0:T(128)S(1)} %dynamic-update-slice.18), channel_id=1, replica_groups=mesh['row_0'=4,'row_1'=4,'row_2'=2,'col_0'=2,'col_1'=4] {'col_0'}, use_global_device_ids=true, to_apply=%add.13 | all-reduce | flops 4 | bytes 32
  268.4 13.9 %all-reduce.20 = (f32[4]{0:T(128)S(1)}, f32[4]{0:T(128)S(1)}) all-reduce(f32[4]{0:T(128)S(1)} %dynamic-update-slice.14, f32[4]{0:T(128)S(1)} %dynamic-update-slice.19), channel_id=1, replica_groups=mesh['row_0'=4,'row_1'=4,'row_2'=2,'col_0'=2,'col_1'=4] {'col_1'}, use_global_device_ids=true, to_apply=%add.14 | all-reduce | flops 8 | bytes 64
  (128 shorter events, 77.2 us)
Async XLA Ops:
  5.8 18.4 %copy-start = (bf16[81,64,256]{2,1,0:T(8,128)(2,1)S(1)}, bf16[81,64,256]{2,1,0:T(8,128)(2,1)}, u32[]{:S(2)}) copy-start(bf16[81,64,256]{2,1,0:T(8,128)(2,1)} %param.1) | copy-start | bytes 7962628
  5.8 9.1 %collective-permute-start = (bf16[81,64,13]{0,1,2:T(8,128)(2,1)S(1)}, bf16[81,64,13]{0,1,2:T(8,128)(2,1)S(1)}, u32[]{:S(2)}, u32[]{:S(2)}) collective-permute-start(bf16[81,64,13]{0,1,2:T(8,128)(2,1)S(1)} %copy.7), channel_id=1, source_target_pairs={{0,1},{1,2},{2,3},{3,4},{4,5},{5,6},{6,7},{8,9},{9,10},{10,11},{11... | collective-permute-start | bytes 404360 | tf_op jit(solution)/shard_map/ppermute | solution.py:26
  12.3 8.6 %collective-permute-start.1 = (bf16[81,64,13]{0,1,2:T(8,128)(2,1)S(1)}, bf16[81,64,13]{0,1,2:T(8,128)(2,1)S(1)}, u32[]{:S(2)}, u32[]{:S(2)}) collective-permute-start(bf16[81,64,13]{0,1,2:T(8,128)(2,1)S(1)} %copy.8), channel_id=1, source_target_pairs={{1,0},{2,1},{3,2},{4,3},{5,4},{6,5},{7,6},{9,8},{10,9},{11,10},{12... | collective-permute-start | bytes 404360 | tf_op jit(solution)/shard_map/ppermute | solution.py:27
  24.1 4.3 %copy-start.1 = (bf16[81,64,13]{2,1,0:T(8,128)(2,1)S(1)}, bf16[81,64,13]{2,1,0:T(8,128)(2,1)}, u32[]{:S(2)}) copy-start(bf16[81,64,13]{2,1,0:T(8,128)(2,1)} %copy.5) | copy-start | bytes 404356
  24.1 4.3 %copy-start.2 = (bf16[81,64,13]{2,1,0:T(8,128)(2,1)S(1)}, bf16[81,64,13]{2,1,0:T(8,128)(2,1)}, u32[]{:S(2)}) copy-start(bf16[81,64,13]{2,1,0:T(8,128)(2,1)} %copy.6) | copy-start | bytes 404356
  29.5 16.1 %collective-permute-start.3 = (bf16[9,1,282]{2,1,0:T(2,128)(2,1)S(1)}, bf16[9,1,282]{2,1,0:T(2,128)(2,1)S(1)}, u32[]{:S(2)}, u32[]{:S(2)}) collective-permute-start(bf16[9,1,282]{2,1,0:T(2,128)(2,1)S(1)} %get-tuple-element.121), channel_id=1, source_target_pairs={{0,8},{8,16},{16,24},{24,32},{32,40},{40,48},{48,56},{56,64},{64,7... | collective-permute-start | bytes 15236 | tf_op jit(solution)/shard_map/ppermute | solution.py:26
  31.5 16.3 %collective-permute-start.4 = (bf16[9,1,282]{2,1,0:T(2,128)(2,1)S(1)}, bf16[9,1,282]{2,1,0:T(2,128)(2,1)S(1)}, u32[]{:S(2)}, u32[]{:S(2)}) collective-permute-start(bf16[9,1,282]{2,1,0:T(2,128)(2,1)S(1)} %get-tuple-element.122), channel_id=1, source_target_pairs={{8,0},{16,8},{24,16},{32,24},{40,32},{48,40},{56,48},{64,56},{72,6... | collective-permute-start | bytes 15236 | tf_op jit(solution)/shard_map/ppermute | solution.py:27
  37.9 27.5 %collective-permute-start.11 = (bf16[9,13,282]{2,1,0:T(8,128)(2,1)S(1)}, bf16[9,13,282]{2,1,0:T(8,128)(2,1)S(1)}, u32[]{:S(2)}, u32[]{:S(2)}) collective-permute-start(bf16[9,13,282]{2,1,0:T(8,128)(2,1)S(1)} %get-tuple-element.113), channel_id=1, source_target_pairs={{8,0},{16,8},{24,16},{32,24},{40,32},{48,40},{56,48},{64,56},{72,6... | collective-permute-start | bytes 197972 | tf_op jit(solution)/shard_map/ppermute | solution.py:27
  40.0 21.7 %collective-permute-start.10 = (bf16[9,10,282]{2,1,0:T(8,128)(2,1)S(1)}, bf16[9,10,282]{2,1,0:T(8,128)(2,1)S(1)}, u32[]{:S(2)}, u32[]{:S(2)}) collective-permute-start(bf16[9,10,282]{2,1,0:T(8,128)(2,1)S(1)} %get-tuple-element.115), channel_id=1, source_target_pairs={{8,0},{16,8},{24,16},{32,24},{40,32},{48,40},{56,48},{64,56},{72,6... | collective-permute-start | bytes 152288 | tf_op jit(solution)/shard_map/ppermute | solution.py:27
  43.7 14.0 %collective-permute-start.9 = (bf16[9,7,282]{2,1,0:T(8,128)(2,1)S(1)}, bf16[9,7,282]{2,1,0:T(8,128)(2,1)S(1)}, u32[]{:S(2)}, u32[]{:S(2)}) collective-permute-start(bf16[9,7,282]{2,1,0:T(8,128)(2,1)S(1)} %get-tuple-element.117), channel_id=1, source_target_pairs={{8,0},{16,8},{24,16},{32,24},{40,32},{48,40},{56,48},{64,56},{72,6... | collective-permute-start | bytes 106604 | tf_op jit(solution)/shard_map/ppermute | solution.py:27
  45.6 4.9 %collective-permute-start.8 = (bf16[9,4,282]{2,1,0:T(4,128)(2,1)S(1)}, bf16[9,4,282]{2,1,0:T(4,128)(2,1)S(1)}, u32[]{:S(2)}, u32[]{:S(2)}) collective-permute-start(bf16[9,4,282]{2,1,0:T(4,128)(2,1)S(1)} %get-tuple-element.119), channel_id=1, source_target_pairs={{8,0},{16,8},{24,16},{32,24},{40,32},{48,40},{56,48},{64,56},{72,6... | collective-permute-start | bytes 60920 | tf_op jit(solution)/shard_map/ppermute | solution.py:27
  47.8 7.9 %collective-permute-start.7 = (bf16[9,4,282]{2,1,0:T(4,128)(2,1)S(1)}, bf16[9,4,282]{2,1,0:T(4,128)(2,1)S(1)}, u32[]{:S(2)}, u32[]{:S(2)}) collective-permute-start(bf16[9,4,282]{2,1,0:T(4,128)(2,1)S(1)} %get-tuple-element.120), channel_id=1, source_target_pairs={{0,8},{8,16},{16,24},{24,32},{32,40},{40,48},{48,56},{56,64},{64,7... | collective-permute-start | bytes 60920 | tf_op jit(solution)/shard_map/ppermute | solution.py:26
  50.6 10.2 %collective-permute-start.6 = (bf16[9,7,282]{2,1,0:T(8,128)(2,1)S(1)}, bf16[9,7,282]{2,1,0:T(8,128)(2,1)S(1)}, u32[]{:S(2)}, u32[]{:S(2)}) collective-permute-start(bf16[9,7,282]{2,1,0:T(8,128)(2,1)S(1)} %get-tuple-element.118), channel_id=1, source_target_pairs={{0,8},{8,16},{16,24},{24,32},{32,40},{40,48},{48,56},{56,64},{64,7... | collective-permute-start | bytes 106604 | tf_op jit(solution)/shard_map/ppermute | solution.py:26
  55.6 8.8 %collective-permute-start.5 = (bf16[9,10,282]{2,1,0:T(8,128)(2,1)S(1)}, bf16[9,10,282]{2,1,0:T(8,128)(2,1)S(1)}, u32[]{:S(2)}, u32[]{:S(2)}) collective-permute-start(bf16[9,10,282]{2,1,0:T(8,128)(2,1)S(1)} %get-tuple-element.116), channel_id=1, source_target_pairs={{0,8},{8,16},{16,24},{24,32},{32,40},{40,48},{48,56},{56,64},{64,7... | collective-permute-start | bytes 152288 | tf_op jit(solution)/shard_map/ppermute | solution.py:26
  57.7 8.8 %collective-permute-start.2 = (bf16[9,13,282]{2,1,0:T(8,128)(2,1)S(1)}, bf16[9,13,282]{2,1,0:T(8,128)(2,1)S(1)}, u32[]{:S(2)}, u32[]{:S(2)}) collective-permute-start(bf16[9,13,282]{2,1,0:T(8,128)(2,1)S(1)} %get-tuple-element.114), channel_id=1, source_target_pairs={{0,8},{8,16},{16,24},{24,32},{32,40},{40,48},{48,56},{56,64},{64,7... | collective-permute-start | bytes 197972 | tf_op jit(solution)/shard_map/ppermute | solution.py:26
  102.3 10.9 %collective-permute-start.12 = (f32[1,256]{1,0:T(1,128)S(1)}, f32[1,256]{1,0:T(1,128)S(1)}, u32[]{:S(2)}, u32[]{:S(2)}) collective-permute-start(f32[1,256]{1,0:T(1,128)S(1)} %get-tuple-element.222), channel_id=1, source_target_pairs={{0,8},{8,16},{16,24},{24,32},{32,40},{40,48},{48,56},{56,64},{64,7... | collective-permute-start | bytes 3080 | tf_op jit(solution)/shard_map/ppermute | solution.py:26
  104.2 8.9 %collective-permute-start.13 = (f32[1,256]{1,0:T(1,128)S(1)}, f32[1,256]{1,0:T(1,128)S(1)}, u32[]{:S(2)}, u32[]{:S(2)}) collective-permute-start(f32[1,256]{1,0:T(1,128)S(1)} %get-tuple-element.221), channel_id=1, source_target_pairs={{8,0},{16,8},{24,16},{32,24},{40,32},{48,40},{56,48},{64,56},{72,6... | collective-permute-start | bytes 3080 | tf_op jit(solution)/shard_map/ppermute | solution.py:27
  113.2 11.2 %collective-permute-start.14 = (f32[66,1]{1,0:T(8,128)S(1)}, f32[66,1]{1,0:T(8,128)S(1)}, u32[]{:S(2)}, u32[]{:S(2)}) collective-permute-start(f32[66,1]{1,0:T(8,128)S(1)} %get-tuple-element.217), channel_id=1, source_target_pairs={{1,0},{2,1},{3,2},{4,3},{5,4},{6,5},{7,6},{9,8},{10,9},{11,10},{12... | collective-permute-start | bytes 800 | tf_op jit(solution)/shard_map/ppermute | solution.py:27
  115.7 8.8 %collective-permute-start.15 = (f32[66,1]{1,0:T(8,128)S(1)}, f32[66,1]{1,0:T(8,128)S(1)}, u32[]{:S(2)}, u32[]{:S(2)}) collective-permute-start(f32[66,1]{1,0:T(8,128)S(1)} %get-tuple-element.218), channel_id=1, source_target_pairs={{0,1},{1,2},{2,3},{3,4},{4,5},{5,6},{6,7},{8,9},{9,10},{10,11},{11... | collective-permute-start | bytes 800 | tf_op jit(solution)/shard_map/ppermute | solution.py:26
  142.4 66.9 %collective-permute-start.16 = (f32[1,256]{1,0:T(1,128)S(1)}, f32[1,256]{1,0:T(1,128)S(1)}, u32[]{:S(2)}, u32[]{:S(2)}) collective-permute-start(f32[1,256]{1,0:T(1,128)S(1)} %get-tuple-element.220), channel_id=1, source_target_pairs={{0,8},{8,16},{16,24},{24,32},{32,40},{40,48},{48,56},{56,64},{64,7... | collective-permute-start | bytes 3080 | tf_op jit(solution)/shard_map/ppermute | solution.py:26
  157.8 51.5 %collective-permute-start.17 = (f32[1,256]{1,0:T(1,128)S(1)}, f32[1,256]{1,0:T(1,128)S(1)}, u32[]{:S(2)}, u32[]{:S(2)}) collective-permute-start(f32[1,256]{1,0:T(1,128)S(1)} %get-tuple-element.219), channel_id=1, source_target_pairs={{8,0},{16,8},{24,16},{32,24},{40,32},{48,40},{56,48},{64,56},{72,6... | collective-permute-start | bytes 3080 | tf_op jit(solution)/shard_map/ppermute | solution.py:27
  209.4 8.4 %collective-permute-start.18 = (f32[66,1]{1,0:T(8,128)S(1)}, f32[66,1]{1,0:T(8,128)S(1)}, u32[]{:S(2)}, u32[]{:S(2)}) collective-permute-start(f32[66,1]{1,0:T(8,128)S(1)} %get-tuple-element.215), channel_id=1, source_target_pairs={{1,0},{2,1},{3,2},{4,3},{5,4},{6,5},{7,6},{9,8},{10,9},{11,10},{12... | collective-permute-start | bytes 800 | tf_op jit(solution)/shard_map/ppermute | solution.py:27
  212.5 5.9 %collective-permute-start.19 = (f32[66,1]{1,0:T(8,128)S(1)}, f32[66,1]{1,0:T(8,128)S(1)}, u32[]{:S(2)}, u32[]{:S(2)}) collective-permute-start(f32[66,1]{1,0:T(8,128)S(1)} %get-tuple-element.216), channel_id=1, source_target_pairs={{0,1},{1,2},{2,3},{3,4},{4,5},{5,6},{6,7},{8,9},{9,10},{10,11},{11... | collective-permute-start | bytes 800 | tf_op jit(solution)/shard_map/ppermute | solution.py:26
